TPU v7x, 256 devices: a whole 4x4x8 slice. The times are simulated.
256 devices in a mesh: band: 64 (over x, z, y_hi), grid: 4 (over y_lo, core).
Axes of the slice: x: 4, y: 4 (y_hi: 2, y_lo: 2; y = y_hi * 2 + y_lo), z: 8, core: 2. Of those that a mesh axis runs over, the one named last changes fastest.
Arguments:
- orbitals: float32 [64, 128, 128, 128], P('band', 'grid'), may hold values from -4.6 to 4.6
Outputs:
- exchange_out: float32 [64, 128, 128, 128], P('band', 'grid')
All inputs are finite; a program needn't handle non-finite values.
Results may differ from a plain program's by a relative error of at most 0.0003.
Values sent between devices are 32-bit elements; how exact they have to be, the bound alone decides.
A program may use at most 128 MiB of HBM per device.

v0:
```python
import math

import jax
import jax.numpy as jnp
from jax import lax
from jax.sharding import PartitionSpec as P


def shifted(x, axis, by):
    size = lax.axis_size(axis)
    return lax.ppermute(x, axis, [(i, (i + by) % size) for i in range(size)])


def cas_matrix(points):
    positions = jnp.arange(points, dtype=jnp.int32)
    phase = positions[:, None] * positions[None, :] % points
    angles = 2.0 * math.pi / points * phase.astype(jnp.float32)
    return jnp.cos(angles) + jnp.sin(angles)


def wrapped_index(positions, points):
    return jnp.minimum(positions, points - positions).astype(jnp.float32)


def make_kernel(points, rows_y, first_y):
    wave_x = wrapped_index(jnp.arange(points, dtype=jnp.int32), points)
    wave_y = wrapped_index(first_y + jnp.arange(rows_y, dtype=jnp.int32), points)
    denominator = (
        wave_x[:, None, None] ** 2 + wave_y[None, :, None] ** 2 + wave_x[None, None, :] ** 2
    )
    strength = points * math.sqrt(points) / 16.0 / float(points**3)
    return jnp.where(denominator > 0, strength / jnp.maximum(denominator, 1.0), 0.0)


def potentials(densities, cas_table, kernel):
    highest = lax.Precision.HIGHEST
    sectioned = jnp.einsum("pxyz,zk->pxyk", densities, cas_table, precision=highest)
    sectioned = jnp.einsum("pxyz,yk->pxkz", sectioned, cas_table, precision=highest)
    spectrum = (
        jnp.einsum(
            "pxyz,xk->pkyz",
            lax.all_to_all(sectioned, "grid", split_axis=2, concat_axis=1, tiled=True),
            cas_table,
            precision=highest,
        )
        * kernel
    )
    spectrum = jnp.einsum("pxyz,xk->pkyz", spectrum, cas_table, precision=highest)
    mixed = lax.all_to_all(spectrum, "grid", split_axis=1, concat_axis=2, tiled=True)
    mixed = jnp.einsum("pxyz,yk->pxkz", mixed, cas_table, precision=highest)
    return jnp.einsum("pxyz,zk->pxyk", mixed, cas_table, precision=highest)


def pair_block(local_block, partner, cas_table, kernel):
    count = local_block.shape[0]
    densities = (local_block[:, None] * partner[None, :]).reshape(
        (count * count,) + local_block.shape[1:]
    )
    return potentials(densities, cas_table, kernel).reshape((count, count) + local_block.shape[1:])


def fetch_blocks(local_block, direction):
    near = shifted(local_block, "band", direction)
    far = shifted(near, "band", direction)
    return (near, far)


def on_device(orbitals):
    points = orbitals.shape[2]
    rows_y = points // lax.axis_size("grid")
    cas_table = cas_matrix(points)
    kernel = make_kernel(points, rows_y, lax.axis_index("grid") * rows_y)
    own_potential = pair_block(orbitals, orbitals, cas_table, kernel)
    accumulated = jnp.sum(own_potential * orbitals[None], axis=1)
    below_near, below_far = fetch_blocks(orbitals, 1)
    above_near, above_far = fetch_blocks(orbitals, -1)
    for partner in (below_near, below_far, above_near, above_far):
        potential_block = pair_block(orbitals, partner, cas_table, kernel)
        accumulated = accumulated + jnp.sum(potential_block * partner[None], axis=1)
    return -accumulated


def solution(mesh):
    in_specs = (P("band", "grid", None, None),)
    out_specs = P("band", "grid", None, None)
    return jax.shard_map(
        on_device, mesh=mesh, in_specs=in_specs, out_specs=out_specs, check_vma=False
    )
```

profile of v0, /device:TPU:1, one launch (start us, length us, event | category | flops | bytes accessed | tf_op | source)
XLA Modules:
  0.0 502.8 jit_solution(16555195263214769128)
XLA Ops:
  8.5 7.8 %all-to-all-start = ((f32[1,32,128,128]{3,1,0,2:T(8,128)}), f32[1,32,128,128]{3,1,0,2:T(8,128)}, u32[]{:S(2)}, u32[]{:S(2)}) async-start(f32[1,32,128,128]{3,1,0,2:T(8,128)} %copy.88), calls=%async_computation | async-start | bytes 4194304 | tf_op jit(solution)/shard_map/all_to_all | solution.py:42
  16.3 8.9 %collective-permute-start.2 = (f32[1,32,128,128]{3,2,1,0:T(8,128)S(1)}, f32[1,32,128,128]{3,2,1,0:T(8,128)}, u32[]{:S(2)}, u32[]{:S(2)}) collective-permute-start(f32[1,32,128,128]{3,2,1,0:T(8,128)S(1)} %copy-done), channel_id=1, source_target_pairs={{0,252},{4,0},{8,4},{12,8},{16,12},{20,16},{24,20},{28,24},{32,28}... | collective-permute-start | bytes 6291464 | tf_op jit(solution)/shard_map/ppermute | solution.py:11
  25.3 60.9 %all-to-all-done = f32[1,32,128,128]{3,1,0,2:T(8,128)} async-done(((f32[1,32,128,128]{3,1,0,2:T(8,128)}), f32[1,32,128,128]{3,1,0,2:T(8,128)}, u32[]{:S(2)}, u32[]{:S(2)}) %all-to-all-start) | async-done | bytes 2097184 | tf_op jit(solution)/shard_map/all_to_all | solution.py:42
  97.7 5.3 %all-to-all-start.1 = ((f32[1,128,32,128]{3,2,0,1:T(8,128)}), f32[1,128,32,128]{3,2,0,1:T(8,128)}, u32[]{:S(2)}, u32[]{:S(2)}) async-start(f32[1,128,32,128]{3,2,0,1:T(8,128)} %copy.94), calls=%async_computation.1 | async-start | bytes 4194304 | tf_op jit(solution)/shard_map/all_to_all | solution.py:49
  112.0 15.9 %all-to-all-done.1 = f32[1,128,32,128]{3,2,0,1:T(8,128)} async-done(((f32[1,128,32,128]{3,2,0,1:T(8,128)}), f32[1,128,32,128]{3,2,0,1:T(8,128)}, u32[]{:S(2)}, u32[]{:S(2)}) %all-to-all-start.1) | async-done | bytes 2097184 | tf_op jit(solution)/shard_map/all_to_all | solution.py:49
  128.0 5.8 %all-to-all-start.6 = ((f32[1,32,128,128]{3,1,0,2:T(8,128)}), f32[1,32,128,128]{3,1,0,2:T(8,128)}, u32[]{:S(2)}, u32[]{:S(2)}) async-start(f32[1,32,128,128]{3,1,0,2:T(8,128)} %copy.118), calls=%async_computation.6 | async-start | bytes 4194304 | tf_op jit(solution)/shard_map/all_to_all | solution.py:42
  133.7 37.2 %collective-permute-done = f32[1,32,128,128]{3,2,1,0:T(8,128)} collective-permute-done((f32[1,32,128,128]{3,2,1,0:T(8,128)S(1)}, f32[1,32,128,128]{3,2,1,0:T(8,128)}, u32[]{:S(2)}, u32[]{:S(2)}) %collective-permute-start) | collective-permute-done | bytes 2097184 | tf_op jit(solution)/shard_map/ppermute | solution.py:11
  179.4 16.0 %all-to-all-done.6 = f32[1,32,128,128]{3,1,0,2:T(8,128)} async-done(((f32[1,32,128,128]{3,1,0,2:T(8,128)}), f32[1,32,128,128]{3,1,0,2:T(8,128)}, u32[]{:S(2)}, u32[]{:S(2)}) %all-to-all-start.6) | async-done | bytes 2097184 | tf_op jit(solution)/shard_map/all_to_all | solution.py:42
  195.4 5.5 %all-to-all-start.2 = ((f32[1,32,128,128]{3,1,0,2:T(8,128)}), f32[1,32,128,128]{3,1,0,2:T(8,128)}, u32[]{:S(2)}, u32[]{:S(2)}) async-start(f32[1,32,128,128]{3,1,0,2:T(8,128)} %copy.98), calls=%async_computation.2 | async-start | bytes 4194304 | tf_op jit(solution)/shard_map/all_to_all | solution.py:42
  212.3 13.4 %all-to-all-done.2 = f32[1,32,128,128]{3,1,0,2:T(8,128)} async-done(((f32[1,32,128,128]{3,1,0,2:T(8,128)}), f32[1,32,128,128]{3,1,0,2:T(8,128)}, u32[]{:S(2)}, u32[]{:S(2)}) %all-to-all-start.2) | async-done | bytes 2097184 | tf_op jit(solution)/shard_map/all_to_all | solution.py:42
  225.7 5.3 %all-to-all-start.7 = ((f32[1,128,32,128]{3,2,0,1:T(8,128)}), f32[1,128,32,128]{3,2,0,1:T(8,128)}, u32[]{:S(2)}, u32[]{:S(2)}) async-start(f32[1,128,32,128]{3,2,0,1:T(8,128)} %copy.124), calls=%async_computation.7 | async-start | bytes 4194304 | tf_op jit(solution)/shard_map/all_to_all | solution.py:49
  242.7 58.5 %all-to-all-done.7 = f32[1,128,32,128]{3,2,0,1:T(8,128)} async-done(((f32[1,128,32,128]{3,2,0,1:T(8,128)}), f32[1,128,32,128]{3,2,0,1:T(8,128)}, u32[]{:S(2)}, u32[]{:S(2)}) %all-to-all-start.7) | async-done | bytes 2097184 | tf_op jit(solution)/shard_map/all_to_all | solution.py:49
  301.2 4.9 all-to-all-start.3
  314.9 16.1 %all-to-all-done.3 = f32[1,128,32,128]{3,2,0,1:T(8,128)} async-done(((f32[1,128,32,128]{3,2,0,1:T(8,128)}), f32[1,128,32,128]{3,2,0,1:T(8,128)}, u32[]{:S(2)}, u32[]{:S(2)}) %all-to-all-start.3) | async-done | bytes 2097184 | tf_op jit(solution)/shard_map/all_to_all | solution.py:49
  331.0 5.8 %all-to-all-start.8 = ((f32[1,32,128,128]{3,1,0,2:T(8,128)}), f32[1,32,128,128]{3,1,0,2:T(8,128)}, u32[]{:S(2)}, u32[]{:S(2)}) async-start(f32[1,32,128,128]{3,1,0,2:T(8,128)} %copy.128), calls=%async_computation.8 | async-start | bytes 4194304 | tf_op jit(solution)/shard_map/all_to_all | solution.py:42
  336.8 37.3 %collective-permute-done.1 = f32[1,32,128,128]{3,2,1,0:T(8,128)} collective-permute-done((f32[1,32,128,128]{3,2,1,0:T(8,128)}, f32[1,32,128,128]{3,2,1,0:T(8,128)}, u32[]{:S(2)}, u32[]{:S(2)}) %collective-permute-start.1) | collective-permute-done | bytes 2097184 | tf_op jit(solution)/shard_map/ppermute | solution.py:11
  382.5 15.9 %all-to-all-done.8 = f32[1,32,128,128]{3,1,0,2:T(8,128)} async-done(((f32[1,32,128,128]{3,1,0,2:T(8,128)}), f32[1,32,128,128]{3,1,0,2:T(8,128)}, u32[]{:S(2)}, u32[]{:S(2)}) %all-to-all-start.8) | async-done | bytes 2097184 | tf_op jit(solution)/shard_map/all_to_all | solution.py:42
  398.4 5.5 %all-to-all-start.4 = ((f32[1,32,128,128]{3,1,0,2:T(8,128)}), f32[1,32,128,128]{3,1,0,2:T(8,128)}, u32[]{:S(2)}, u32[]{:S(2)}) async-start(f32[1,32,128,128]{3,1,0,2:T(8,128)} %copy.108), calls=%async_computation.4 | async-start | bytes 4194304 | tf_op jit(solution)/shard_map/all_to_all | solution.py:42
  415.3 13.4 %all-to-all-done.4 = f32[1,32,128,128]{3,1,0,2:T(8,128)} async-done(((f32[1,32,128,128]{3,1,0,2:T(8,128)}), f32[1,32,128,128]{3,1,0,2:T(8,128)}, u32[]{:S(2)}, u32[]{:S(2)}) %all-to-all-start.4) | async-done | bytes 2097184 | tf_op jit(solution)/shard_map/all_to_all | solution.py:42
  428.8 5.5 %all-to-all-start.9 = ((f32[1,128,32,128]{3,2,0,1:T(8,128)}), f32[1,128,32,128]{3,2,0,1:T(8,128)}, u32[]{:S(2)}, u32[]{:S(2)}) async-start(f32[1,128,32,128]{3,2,0,1:T(8,128)} %copy.134), calls=%async_computation.9 | async-start | bytes 4194304 | tf_op jit(solution)/shard_map/all_to_all | solution.py:49
  460.1 4.5 all-to-all-start.5
  464.6 5.1 %fusion.4 = f32[32,128,128]{2,1,0:T(8,128)} fusion(f32[128,32,128]{2,0,1:T(8,128)} %fusion.86), kind=kOutput, calls=%fused_computation.6 | convolution fusion | flops 805552128 | bytes 4194304 | tf_op jit(solution)/shard_map/pxyz,zk->pxyk/dot_general | solution.py:51
  482.7 6.8 %all-to-all-done.5 = f32[1,128,32,128]{3,2,0,1:T(8,128)} async-done(((f32[1,128,32,128]{3,2,0,1:T(8,128)}), f32[1,128,32,128]{3,2,0,1:T(8,128)}, u32[]{:S(2)}, u32[]{:S(2)}) %all-to-all-start.5) | async-done | bytes 2097184 | tf_op jit(solution)/shard_map/all_to_all | solution.py:49
  496.0 6.6 %fusion.14 = f32[1,32,128,128]{3,2,1,0:T(8,128)} fusion(f32[32,128,128]{2,1,0:T(8,128)S(1)} %copy-done.5, f32[1,32,128,128]{3,2,1,0:T(8,128)} %collective-permute-done.3, f32[32,128,128]{2,1,0:T(8,128)S(1)} %copy-done.3, f32[1,32,128,128]{3,2,1,0:T(8,128)} %collective-permute-done.2, f32[32,128,128]{2,1,0:T(8,128)S(1)} %fusion.6, ...), kind=kOutput, calls=%fused_computation.17 | convolution fusion | flops 810795008 | bytes 23068672 | tf_op jit(solution)/shard_map/pxyz,zk->pxyk/dot_general | solution.py:51
  (74 shorter events, 134.3 us)
Async XLA Ops:
  8.5 7.8 %copy-start = (f32[1,32,128,128]{3,2,1,0:T(8,128)S(1)}, f32[1,32,128,128]{3,2,1,0:T(8,128)}, u32[]{:S(2)}) copy-start(f32[1,32,128,128]{3,2,1,0:T(8,128)} %param.1) | copy-start | bytes 6291460
  8.5 77.7 %all-to-all-start = ((f32[1,32,128,128]{3,1,0,2:T(8,128)}), f32[1,32,128,128]{3,1,0,2:T(8,128)}, u32[]{:S(2)}, u32[]{:S(2)}) async-start(f32[1,32,128,128]{3,1,0,2:T(8,128)} %copy.88), calls=%async_computation | async-start | bytes 4194304 | tf_op jit(solution)/shard_map/all_to_all | solution.py:42
  16.3 87.3 %collective-permute-start.2 = (f32[1,32,128,128]{3,2,1,0:T(8,128)S(1)}, f32[1,32,128,128]{3,2,1,0:T(8,128)}, u32[]{:S(2)}, u32[]{:S(2)}) collective-permute-start(f32[1,32,128,128]{3,2,1,0:T(8,128)S(1)} %copy-done), channel_id=1, source_target_pairs={{0,252},{4,0},{8,4},{12,8},{16,12},{20,16},{24,20},{28,24},{32,28}... | collective-permute-start | bytes 6291464 | tf_op jit(solution)/shard_map/ppermute | solution.py:11
  97.7 30.3 %all-to-all-start.1 = ((f32[1,128,32,128]{3,2,0,1:T(8,128)}), f32[1,128,32,128]{3,2,0,1:T(8,128)}, u32[]{:S(2)}, u32[]{:S(2)}) async-start(f32[1,128,32,128]{3,2,0,1:T(8,128)} %copy.94), calls=%async_computation.1 | async-start | bytes 4194304 | tf_op jit(solution)/shard_map/all_to_all | solution.py:49
  103.0 67.9 %collective-permute-start = (f32[1,32,128,128]{3,2,1,0:T(8,128)S(1)}, f32[1,32,128,128]{3,2,1,0:T(8,128)}, u32[]{:S(2)}, u32[]{:S(2)}) collective-permute-start(f32[1,32,128,128]{3,2,1,0:T(8,128)S(1)} %copy-done), channel_id=1, source_target_pairs={{0,4},{4,8},{8,12},{12,16},{16,20},{20,24},{24,28},{28,32},{32,36}... | collective-permute-start | bytes 6291464 | tf_op jit(solution)/shard_map/ppermute | solution.py:11
  128.0 67.4 %all-to-all-start.6 = ((f32[1,32,128,128]{3,1,0,2:T(8,128)}), f32[1,32,128,128]{3,1,0,2:T(8,128)}, u32[]{:S(2)}, u32[]{:S(2)}) async-start(f32[1,32,128,128]{3,1,0,2:T(8,128)} %copy.118), calls=%async_computation.6 | async-start | bytes 4194304 | tf_op jit(solution)/shard_map/all_to_all | solution.py:42
  195.4 30.4 %all-to-all-start.2 = ((f32[1,32,128,128]{3,1,0,2:T(8,128)}), f32[1,32,128,128]{3,1,0,2:T(8,128)}, u32[]{:S(2)}, u32[]{:S(2)}) async-start(f32[1,32,128,128]{3,1,0,2:T(8,128)} %copy.98), calls=%async_computation.2 | async-start | bytes 4194304 | tf_op jit(solution)/shard_map/all_to_all | solution.py:42
  225.7 75.4 %all-to-all-start.7 = ((f32[1,128,32,128]{3,2,0,1:T(8,128)}), f32[1,128,32,128]{3,2,0,1:T(8,128)}, u32[]{:S(2)}, u32[]{:S(2)}) async-start(f32[1,128,32,128]{3,2,0,1:T(8,128)} %copy.124), calls=%async_computation.7 | async-start | bytes 4194304 | tf_op jit(solution)/shard_map/all_to_all | solution.py:49
  231.0 75.4 %collective-permute-start.3 = (f32[1,32,128,128]{3,2,1,0:T(8,128)}, f32[1,32,128,128]{3,2,1,0:T(8,128)}, u32[]{:S(2)}, u32[]{:S(2)}) collective-permute-start(f32[1,32,128,128]{3,2,1,0:T(8,128)} %collective-permute-done.2), channel_id=1, source_target_pairs={{0,252},{4,0},{8,4},{12,8},{16,12},{20,16},{24,20},{28,24},{32,28}... | collective-permute-start | bytes 6291464 | tf_op jit(solution)/shard_map/ppermute | solution.py:11
  301.2 29.8 %all-to-all-start.3 = ((f32[1,128,32,128]{3,2,0,1:T(8,128)}), f32[1,128,32,128]{3,2,0,1:T(8,128)}, u32[]{:S(2)}, u32[]{:S(2)}) async-start(f32[1,128,32,128]{3,2,0,1:T(8,128)} %copy.104), calls=%async_computation.3 | async-start | bytes 4194304 | tf_op jit(solution)/shard_map/all_to_all | solution.py:49
  306.0 68.0 %collective-permute-start.1 = (f32[1,32,128,128]{3,2,1,0:T(8,128)}, f32[1,32,128,128]{3,2,1,0:T(8,128)}, u32[]{:S(2)}, u32[]{:S(2)}) collective-permute-start(f32[1,32,128,128]{3,2,1,0:T(8,128)} %collective-permute-done), channel_id=1, source_target_pairs={{0,4},{4,8},{8,12},{12,16},{16,20},{20,24},{24,28},{28,32},{32,36}... | collective-permute-start | bytes 6291464 | tf_op jit(solution)/shard_map/ppermute | solution.py:11
  331.0 67.4 %all-to-all-start.8 = ((f32[1,32,128,128]{3,1,0,2:T(8,128)}), f32[1,32,128,128]{3,1,0,2:T(8,128)}, u32[]{:S(2)}, u32[]{:S(2)}) async-start(f32[1,32,128,128]{3,1,0,2:T(8,128)} %copy.128), calls=%async_computation.8 | async-start | bytes 4194304 | tf_op jit(solution)/shard_map/all_to_all | solution.py:42
  398.4 30.4 %all-to-all-start.4 = ((f32[1,32,128,128]{3,1,0,2:T(8,128)}), f32[1,32,128,128]{3,1,0,2:T(8,128)}, u32[]{:S(2)}, u32[]{:S(2)}) async-start(f32[1,32,128,128]{3,1,0,2:T(8,128)} %copy.108), calls=%async_computation.4 | async-start | bytes 4194304 | tf_op jit(solution)/shard_map/all_to_all | solution.py:42
  428.8 31.3 %all-to-all-start.9 = ((f32[1,128,32,128]{3,2,0,1:T(8,128)}), f32[1,128,32,128]{3,2,0,1:T(8,128)}, u32[]{:S(2)}, u32[]{:S(2)}) async-start(f32[1,128,32,128]{3,2,0,1:T(8,128)} %copy.134), calls=%async_computation.9 | async-start | bytes 4194304 | tf_op jit(solution)/shard_map/all_to_all | solution.py:49
  460.1 29.4 %all-to-all-start.5 = ((f32[1,128,32,128]{3,2,0,1:T(8,128)}), f32[1,128,32,128]{3,2,0,1:T(8,128)}, u32[]{:S(2)}, u32[]{:S(2)}) async-start(f32[1,128,32,128]{3,2,0,1:T(8,128)} %copy.114), calls=%async_computation.5 | async-start | bytes 4194304 | tf_op jit(solution)/shard_map/all_to_all | solution.py:49
  464.6 5.1 %copy-start.1 = (f32[1,4,32,32,128]{4,3,1,2,0:T(8,128)S(1)}, f32[1,4,32,32,128]{4,3,1,2,0:T(8,128)}, u32[]{:S(2)}) copy-start(f32[1,4,32,32,128]{4,3,1,2,0:T(8,128)} %copy.105) | copy-start | bytes 6291460
  491.3 4.6 copy-start.4
  491.3 4.6 copy-start.5
  493.7 2.2 copy-start.2
  493.7 2.2 copy-start.3
where the time goes:
time: 509 us; the launch traced here: 503 us
  waiting for transfers between devices  291 us (57%)
  matrix products  93.6 us (18%)
  starting transfers between devices  65.8 us (13%)
  local copies, waits for them, and re-layouts  51.4 us (10%)
    all_to_all x5, waiting for transfers between devices, potentials(): lax.all_to_all(sectioned, 'grid', split_axis=2, concat_axis=1, tiled=True)  120 us
    all_to_all x5, waiting for transfers between devices, potentials(): lax.all_to_all(spectrum, 'grid', split_axis=1, concat_axis=2, tiled=True)  97.3 us
    ppermute x4, waiting for transfers between devices, shifted(): return lax.ppermute(x, axis, [(i, (i + by) % size) for i in range(size)])  74.5 us
    all_to_all x5, starting transfers between devices, potentials(): lax.all_to_all(sectioned, 'grid', split_axis=2, concat_axis=1, tiled=True)  30.3 us
    all_to_all x5, starting transfers between devices, potentials(): lax.all_to_all(spectrum, 'grid', split_axis=1, concat_axis=2, tiled=True)  25.5 us
    dot_general x5, matrix products, potentials(): return jnp.einsum('pxyz,zk->pxyk', mixed, cas_table, precision=highest)  20.6 us
    dot_general x5, matrix products, potentials(): jnp.einsum('pxyz,zk->pxyk', densities, cas_table, precision=highest)  18.5 us
    dot_general x5, matrix products, potentials(): jnp.einsum('pxyz,xk->pkyz', lax.all_to_all(sectioned, 'grid', split_axis=...  16.3 us
  transfers between devices with their start and end apart: 14, of which 11 were waited for; matrix products, arithmetic and copies ran while one was open for 25% of the time, Pallas kernels for 0%

commit v1 on v0

v1 whole, which is shorter than its diff:
```python
import functools
import math

import jax
import jax.numpy as jnp
import ml_dtypes
import numpy as np
from jax import lax
from jax.experimental import pallas as pl
from jax.experimental.pallas import tpu as pltpu
from jax.sharding import PartitionSpec as P

MESH = pl.DeviceIdType.MESH
BF16 = jnp.bfloat16
F32 = jnp.float32
N = 128
Q = 32
H = 64

OH, OX, PH, PX, MH, MX, QH, QX, RH, RX = range(10)
T_OX, T_PX, T_MH, T_QH, T_MX, T_QX, T_PHA, T_PHB = range(8)
T_RX = 8
T_RH = 12
CHUNKS = 4
CH = Q // CHUNKS
T_COUNT = 16
E_OWN, E_OTHER, E_BACK = range(3)


def split(value):
    high = value.astype(BF16)
    low = (value - high.astype(F32)).astype(BF16)
    return high, low


def mm(a, b):
    return jnp.dot(a, b, preferred_element_type=F32)


def stacked(value):
    high, low = split(value)
    return jnp.concatenate([high, low], axis=0)


def kernel(x_ref, wz, wy, wx, wxi, wyi, out_ref, orb, spec, send, ga, gb, back, vt, ssem, rsem, esem, fsem, lsem):
    band = lax.axis_index("band")
    grid = lax.axis_index("grid")
    bands = lax.axis_size("band")
    core = grid % 2
    side = band % 2
    mate = (band, grid + 1 - 2 * core)
    near = (band, (grid + 2) % 4)
    cross = (band + 1 - 2 * side, (grid + 2) % 4)
    up = ((band + 2) % bands, grid)
    down = ((band + bands - 2) % bands, grid)

    own_copy = pltpu.make_async_copy(x_ref.at[0], orb.at[OH], lsem)
    own_copy.start()
    barrier = pltpu.get_barrier_semaphore()
    for other in (mate, near, cross, up, down):
        pl.semaphore_signal(barrier, inc=1, device_id=other, device_id_type=MESH)
    pl.semaphore_wait(barrier, 5)

    def transfer(index, src, dst, device):
        return pltpu.make_async_remote_copy(
            src_ref=src,
            dst_ref=dst,
            send_sem=ssem.at[index],
            recv_sem=rsem.at[index],
            device_id=device,
            device_id_type=MESH,
        )

    passed = jnp.where(side == 0, QH, MH)
    half_q = Q // 2
    moves = {
        T_OX: transfer(T_OX, x_ref.at[0], orb.at[OX], near),
        T_PX: transfer(T_PX, x_ref.at[0], orb.at[PX], cross),
        T_MH: transfer(T_MH, x_ref.at[0], orb.at[MH], up),
        T_QH: transfer(T_QH, x_ref.at[0], orb.at[QH], down),
        T_MX: transfer(T_MX, orb.at[OX], orb.at[MX], up),
        T_QX: transfer(T_QX, orb.at[OX], orb.at[QX], down),
        T_PHA: transfer(T_PHA, orb.at[PX, pl.ds(0, half_q)], orb.at[PH, pl.ds(0, half_q)], near),
        T_PHB: transfer(T_PHB, orb.at[OX, pl.ds(half_q, half_q)], orb.at[PH, pl.ds(half_q, half_q)], cross),
    }
    for k in range(CHUNKS):
        rows = pl.ds(k * CH, CH)
        moves[T_RX + k] = transfer(T_RX + k, orb.at[passed, rows], orb.at[RX, rows], cross)
        moves[T_RH + k] = transfer(T_RH + k, orb.at[RX, rows], orb.at[RH, rows], near)

    own_at = jnp.where(core == 0, 3, 1) * (Q * H)
    other_at = jnp.where(core == 0, 1, 3) * (Q * H)

    def swap(index, src, dst):
        return pltpu.make_async_remote_copy(
            src_ref=src,
            dst_ref=dst,
            send_sem=esem.at[index],
            recv_sem=fsem.at[index],
            device_id=mate,
            device_id_type=MESH,
        )

    swaps = (
        swap(E_OWN, send.at[0], spec.at[pl.ds(own_at, Q * H)]),
        swap(E_OTHER, send.at[1], spec.at[pl.ds(other_at, Q * H)]),
        swap(E_BACK, back, gb),
    )

    def forward(o_slot, j_slot, half):
        def step(i, _):
            a = i * 2
            rho = (orb[o_slot, pl.ds(a, 2)] * orb[j_slot, pl.ds(a, 2)]).reshape(2 * N, N)
            high, low = split(rho)
            t = mm(jnp.concatenate([high, low], axis=1), wz[...])
            t = t[:, :N] + t[:, N:]
            u = mm(wy[core], stacked(jnp.concatenate([t[:N], t[N:]], axis=1)))
            u = u[:N] + u[N:]
            keep = pl.multiple_of((half * 2 * Q + a) * H, 2 * H)
            spec[pl.ds(keep, 2 * H), :] = jnp.concatenate([u[:H, :N], u[:H, N:]], axis=0)
            give = pl.multiple_of(a * H, 2 * H)
            send[half, pl.ds(give, 2 * H), :] = jnp.concatenate([u[H:, :N], u[H:, N:]], axis=0)
            return 0

        lax.fori_loop(0, Q // 2, step, 0)
        swaps[half].start()

    def along_x():
        column = spec[pl.ds(0, N, stride=H), :]
        spec[pl.ds(0, N, stride=H), :] = column - jnp.where(zero_mode, jnp.mean(column, axis=0, keepdims=True), 0.0)

        def step(i, _):
            k = i * 2
            m = jnp.concatenate(
                [spec[pl.ds(k, N, stride=H), :], spec[pl.ds(k + 1, N, stride=H), :]], axis=1
            )
            s = mm(wx[...], stacked(m))
            v = jnp.concatenate(
                [vt[pl.ds(pl.multiple_of(k * N, N), N), :], vt[pl.ds(pl.multiple_of(k * N + N, N), N), :]], axis=1
            )
            s = (s[:N] + s[N:]) * v
            r = mm(wxi[core], stacked(s))
            r = r[:H] + r[H:]
            ga[pl.ds(k, Q, stride=H), :] = r[:Q, :N]
            ga[pl.ds(k + 1, Q, stride=H), :] = r[:Q, N:]
            back[pl.ds(k, Q, stride=H), :] = r[Q:, :N]
            back[pl.ds(k + 1, Q, stride=H), :] = r[Q:, N:]
            return 0

        lax.fori_loop(0, H // 2, step, 0)
        swaps[E_BACK].start()

    def inverse(j_slot, first):
        def step(i, _):
            a = i * 2
            rows = pl.ds(pl.multiple_of(a * H, 2 * H), 2 * H)
            mine, theirs = ga[rows, :], gb[rows, :]
            g = jnp.concatenate(
                [
                    jnp.concatenate([mine[:H], mine[H:]], axis=1),
                    jnp.concatenate([theirs[:H], theirs[H:]], axis=1),
                ],
                axis=0,
            )
            t = mm(wyi[core], stacked(g))
            t = t[:N] + t[N:]
            high, low = split(jnp.concatenate([t[:, :N], t[:, N:]], axis=0))
            w = mm(jnp.concatenate([high, low], axis=1), wz[...])
            w = (w[:, :N] + w[:, N:]).reshape(2, N, N) * orb[j_slot, pl.ds(a, 2)]
            if first:
                out_ref[0, pl.ds(a, 2)] = -w
            else:
                out_ref[0, pl.ds(a, 2)] -= w
            return 0

        lax.fori_loop(0, Q // 2, step, 0)

    def finish(j_slot, first=False):
        swaps[E_OWN].wait()
        swaps[E_OTHER].wait()
        along_x()
        swaps[E_BACK].wait()
        inverse(j_slot, first)

    for t in (T_OX, T_PX, T_MH, T_QH):
        moves[t].start()

    strength = N * math.sqrt(N) / 16.0 / float(N**3)
    row = lax.broadcasted_iota(jnp.int32, (N, N), 0)
    column = lax.broadcasted_iota(jnp.int32, (N, N), 1)
    row = jnp.minimum(row, N - row)
    column = jnp.minimum(column, N - column)
    plane = row * row + column * column

    zero_mode = jnp.logical_and(lax.broadcasted_iota(jnp.int32, (1, N), 1) == 0, core == 0)

    def table(i, _):
        ky = core * H + i
        ky = jnp.minimum(ky, N - ky)
        d = (plane + ky * ky).astype(F32)
        vt[pl.ds(pl.multiple_of(i * N, N), N), :] = jnp.where(d > 0, strength / jnp.maximum(d, 1.0), 0.0)
        return 0

    lax.fori_loop(0, H, table, 0)
    own_copy.wait()
    forward(OH, OH, 0)

    moves[T_OX].wait_recv()
    for t in (T_MX, T_QX, T_PHB):
        moves[t].start()
    moves[T_PX].wait_recv()
    moves[T_PHA].start()
    moves[T_MH].wait_recv()
    moves[T_QH].wait_recv()
    for k in range(CHUNKS):
        moves[T_RX + k].start()
    forward(OX, OX, 1)
    finish(OH, first=True)

    def pass_on(k):
        moves[T_RX + k].wait_recv()
        moves[T_RH + k].start()

    moves[T_PHA].wait_recv()
    forward(OX, PX, 1)
    moves[T_PHB].wait_recv()
    pass_on(0)
    forward(OH, PH, 0)
    finish(PH)
    pass_on(1)
    forward(OH, MH, 0)
    moves[T_MX].wait_recv()
    forward(OX, MX, 1)
    finish(MH)
    pass_on(2)
    forward(OH, QH, 0)
    moves[T_QX].wait_recv()
    forward(OX, QX, 1)
    pass_on(3)
    finish(QH)
    forward(OX, RX, 1)
    for k in range(CHUNKS):
        moves[T_RH + k].wait_recv()
    forward(OH, RH, 0)
    finish(RH)
    for t in range(T_COUNT):
        moves[t].wait_send()


def halves(matrix):
    high = matrix.astype(ml_dtypes.bfloat16)
    low = (matrix - high.astype(np.float64)).astype(ml_dtypes.bfloat16)
    return high, low


def left_weight(matrix):
    high, low = halves(matrix)
    return np.concatenate(
        [np.concatenate([high, high], axis=1), np.concatenate([low, np.zeros_like(low)], axis=1)], axis=0
    )


def tables():
    index = np.arange(N)
    angle = 2.0 * np.pi / N * (index[:, None] * index[None, :] % N)
    cas = np.cos(angle) + np.sin(angle)
    high, low = halves(cas)
    wz = np.concatenate(
        [np.concatenate([high, low], axis=1), np.concatenate([high, np.zeros_like(low)], axis=1)], axis=0
    )
    order = [np.concatenate([index[c * H : c * H + H], index[H - c * H : N - c * H]]) for c in (0, 1)]
    wy = np.stack([left_weight(cas[order[c]]) for c in (0, 1)])
    wyi = np.stack([left_weight(cas[:, order[c]]) for c in (0, 1)])
    wx = left_weight(cas)
    kept = [np.concatenate([index[:Q], index[Q : 2 * Q]]), np.concatenate([index[:Q], index[3 * Q :]])]
    wxi = np.stack([left_weight(cas[kept[c]]) for c in (0, 1)])
    return wz, wy, wx, wxi, wyi


def on_device(orbitals):
    weights = [jnp.asarray(w) for w in tables()]
    vmem = pl.BlockSpec(memory_space=pltpu.VMEM)
    return pl.pallas_call(
        kernel,
        out_shape=jax.ShapeDtypeStruct(orbitals.shape, F32),
        in_specs=[pl.BlockSpec(memory_space=pl.ANY)] + [vmem] * 5,
        out_specs=vmem,
        scratch_shapes=[
            pltpu.VMEM((10, Q, N, N), F32),
            pltpu.VMEM((N * H, N), F32),
            pltpu.VMEM((2, Q * H, N), F32),
            pltpu.VMEM((Q * H, N), F32),
            pltpu.VMEM((Q * H, N), F32),
            pltpu.VMEM((Q * H, N), F32),
            pltpu.VMEM((H * N, N), F32),
            pltpu.SemaphoreType.DMA((T_COUNT,)),
            pltpu.SemaphoreType.DMA((T_COUNT,)),
            pltpu.SemaphoreType.DMA((3,)),
            pltpu.SemaphoreType.DMA((3,)),
            pltpu.SemaphoreType.DMA,
        ],
        compiler_params=pltpu.CompilerParams(
            collective_id=0, has_side_effects=True, vmem_limit_bytes=56 * 1024 * 1024
        ),
    )(orbitals, *weights)


def solution(mesh):
    spec = P("band", "grid", None, None)
    return jax.shard_map(on_device, mesh=mesh, in_specs=(spec,), out_specs=spec, check_vma=False)
```

time: 509 us -> 254 us (0.50); the launches traced: 503 us -> 254 us
  waiting for transfers between devices: 291 us -> 0 us
  Pallas kernels: 0 us -> 251 us
  matrix products: 93.6 us -> 0 us
  starting transfers between devices: 65.8 us -> 0 us
  local copies, waits for them, and re-layouts: 51.4 us -> 3.14 us
    pallas_call x0 -> x1, Pallas kernels: none -> 251 us  [on_device(): pl.pallas_call(kernel, out_shape=jax.ShapeDtypeStruct(orbitals.shape, F32...]
    all_to_all x10 -> x0, waiting for transfers between devices: 217 us -> none  [the longest x5 120 us: potentials(): lax.all_to_all(sectioned, 'grid', split_axis=2, concat_axis=1, tiled=True)]
    dot_general x30 -> x0, matrix products: 93.6 us -> none  [the longest x5 20.6 us: potentials(): return jnp.einsum('pxyz,zk->pxyk', mixed, cas_table, precision=highest)]
    ppermute x4 -> x0, waiting for transfers between devices: 74.5 us -> none  [shifted(): return lax.ppermute(x, axis, [(i, (i + by) % size) for i in range(size)])]
    all_to_all x10 -> x0, starting transfers between devices: 55.8 us -> none  [the longest x5 30.3 us: potentials(): lax.all_to_all(sectioned, 'grid', split_axis=2, concat_axis=1, tiled=True)]
    transpose x10 -> x0, local copies, waits for them, and re-layouts: 25.8 us -> none  [the longest x5 13.1 us: potentials(): jnp.einsum('pxyz,xk->pkyz', spectrum, cas_table, precision=highest)]
    all_to_all x15 -> x0, local copies, waits for them, and re-layouts: 25.5 us -> none  [the longest x10 15.1 us: potentials(): lax.all_to_all(sectioned, 'grid', split_axis=2, concat_axis=1, tiled=True)]
    ppermute x4 -> x0, starting transfers between devices: 10 us -> none  [shifted(): return lax.ppermute(x, axis, [(i, (i + by) % size) for i in range(size)])]
  transfers between devices with their start and end apart: 14 -> 0, of which waited for: 11 -> 0; matrix products, arithmetic and copies ran while one was open for 25% -> 0% of each run, Pallas kernels for 0% -> 0%
where the time goes in v1:
time: 254 us
  Pallas kernels  251 us (99%)
  local copies, waits for them, and re-layouts  3.14 us (1%)
    pallas_call x1, Pallas kernels, on_device(): pl.pallas_call(kernel, out_shape=jax.ShapeDtypeStruct(orbitals.shape, F32...  251 us

profile of v1, /device:TPU:1, one launch (start us, length us, event | category | flops | bytes accessed | tf_op | source)
XLA Modules:
  0.0 254.0 jit_solution(17367443929863937043)
XLA Ops:
  0.0 250.8 %shard_map.64 = f32[1,32,128,128]{3,2,1,0:T(8,128)} custom-call(f32[1,32,128,128]{3,2,1,0:T(8,128)} %x_ref.1, bf16[256,256]{1,0:T(8,128)(2,1)} %constant.10.clone.wz, bf16[2,256,256]{2,1,0:T(8,128)(2,1)} %constant.11.clone.wy, bf16[256,256]{1,0:T(8,128)(2,1)} %constant.12.clone.wx, bf16[2,128,256]{2,1,0:T(8,128)(2,1)} %constant.13.clone.wxi, ...), custom_call_target="tpu_custom_call" | custom-call | tf_op jit(solution)/shard_map/pallas_call | solution.py:283
  250.8 3.1 %copy.8 = f32[1,32,128,128]{3,2,1,0:T(8,128)} copy(f32[1,32,128,128]{3,2,1,0:T(8,128)} %shard_map.64) | data formatting | bytes 4194304

commit v2 on v1

--- a/solution.py
+++ b/solution.py
@@ -22,6 +22,7 @@
 T_RX = 8
 T_RH = 12
 CHUNKS = 4
+UNROLL = 4
 CH = Q // CHUNKS
 T_COUNT = 16
 E_OWN, E_OTHER, E_BACK = range(3)
@@ -116,24 +117,29 @@
             t = t[:, :N] + t[:, N:]
             u = mm(wy[core], stacked(jnp.concatenate([t[:N], t[N:]], axis=1)))
             u = u[:N] + u[N:]
-            keep = pl.multiple_of((half * 2 * Q + a) * H, 2 * H)
-            spec[pl.ds(keep, 2 * H), :] = jnp.concatenate([u[:H, :N], u[:H, N:]], axis=0)
-            give = pl.multiple_of(a * H, 2 * H)
-            send[half, pl.ds(give, 2 * H), :] = jnp.concatenate([u[H:, :N], u[H:, N:]], axis=0)
+            for b in range(2):
+                plane = u[:, b * N : b * N + N]
+                spec[pl.ds(half * 2 * Q * H + a + b, H, stride=Q), :] = plane[:H]
+                send[half, pl.ds(a + b, H, stride=Q), :] = plane[H:]
             return 0
 
-        lax.fori_loop(0, Q // 2, step, 0)
+        lax.fori_loop(0, Q // 2, step, 0, unroll=UNROLL)
         swaps[half].start()
 
+    def row_of(k):
+        return jnp.concatenate(
+            [spec[pl.ds(pl.multiple_of(p * Q * H + k * Q, Q), Q), :] for p in range(4)], axis=0
+        )
+
     def along_x():
-        column = spec[pl.ds(0, N, stride=H), :]
-        spec[pl.ds(0, N, stride=H), :] = column - jnp.where(zero_mode, jnp.mean(column, axis=0, keepdims=True), 0.0)
+        column = row_of(0)
+        column = column - jnp.where(zero_mode, jnp.mean(column, axis=0, keepdims=True), 0.0)
+        for p in range(4):
+            spec[pl.ds(p * Q * H, Q), :] = column[p * Q : p * Q + Q]
 
         def step(i, _):
             k = i * 2
-            m = jnp.concatenate(
-                [spec[pl.ds(k, N, stride=H), :], spec[pl.ds(k + 1, N, stride=H), :]], axis=1
-            )
+            m = jnp.concatenate([row_of(k), row_of(k + 1)], axis=1)
             s = mm(wx[...], stacked(m))
             v = jnp.concatenate(
                 [vt[pl.ds(pl.multiple_of(k * N, N), N), :], vt[pl.ds(pl.multiple_of(k * N + N, N), N), :]], axis=1
@@ -147,7 +153,7 @@
             back[pl.ds(k + 1, Q, stride=H), :] = r[Q:, N:]
             return 0
 
-        lax.fori_loop(0, H // 2, step, 0)
+        lax.fori_loop(0, H // 2, step, 0, unroll=UNROLL)
         swaps[E_BACK].start()
 
     def inverse(j_slot, first):
@@ -173,7 +179,7 @@
                 out_ref[0, pl.ds(a, 2)] -= w
             return 0
 
-        lax.fori_loop(0, Q // 2, step, 0)
+        lax.fori_loop(0, Q // 2, step, 0, unroll=UNROLL)
 
     def finish(j_slot, first=False):
         swaps[E_OWN].wait()

time: 254 us -> 187 us (0.74)
  Pallas kernels: 251 us -> 183 us
    pallas_call x1, Pallas kernels: 251 us -> 183 us  [on_device(): pl.pallas_call(kernel, out_shape=jax.ShapeDtypeStruct(orbitals.shape, F32...]
where the time goes in v2:
time: 187 us
  Pallas kernels  183 us (98%)
  local copies, waits for them, and re-layouts  3.14 us (2%)
    pallas_call x1, Pallas kernels, on_device(): pl.pallas_call(kernel, out_shape=jax.ShapeDtypeStruct(orbitals.shape, F32...  183 us

profile of v2, /device:TPU:1, one launch (start us, length us, event | category | flops | bytes accessed | tf_op | source)
XLA Modules:
  0.0 186.5 jit_solution(5179255988656815270)
XLA Ops:
  0.0 183.4 %shard_map.64 = f32[1,32,128,128]{3,2,1,0:T(8,128)} custom-call(f32[1,32,128,128]{3,2,1,0:T(8,128)} %x_ref.1, bf16[256,256]{1,0:T(8,128)(2,1)} %constant.10.clone.wz, bf16[2,256,256]{2,1,0:T(8,128)(2,1)} %constant.11.clone.wy, bf16[256,256]{1,0:T(8,128)(2,1)} %constant.12.clone.wx, bf16[2,128,256]{2,1,0:T(8,128)(2,1)} %constant.13.clone.wxi, ...), custom_call_target="tpu_custom_call" | custom-call | tf_op jit(solution)/shard_map/pallas_call | solution.py:289
  183.4 3.1 %copy.8 = f32[1,32,128,128]{3,2,1,0:T(8,128)} copy(f32[1,32,128,128]{3,2,1,0:T(8,128)} %shard_map.64) | data formatting | bytes 4194304

commit v3 on v2

v3 whole, which is shorter than its diff:
```python
import functools
import math

import jax
import jax.numpy as jnp
import ml_dtypes
import numpy as np
from jax import lax
from jax.experimental import pallas as pl
from jax.experimental.pallas import tpu as pltpu
from jax.sharding import PartitionSpec as P

MESH = pl.DeviceIdType.MESH
BF16 = jnp.bfloat16
F32 = jnp.float32
N = 128
Q = 32
H = 64

OH, OX, PH, PX, MH, MX, QH, QX, RH, RX = range(10)
PART = 16
CH = 4
CHUNKS = 7
ZROWS = CHUNKS * CH
T_OX, T_PX, T_MH, T_QH, T_MXA, T_MXB, T_QXA, T_QXB, T_PHA, T_PHB, T_RXZ, T_RHZ = range(12)
T_RX = 12
T_RH = T_RX + CHUNKS
T_COUNT = T_RH + CHUNKS
SETS = 3
UNROLL = 8


def split(value):
    high = value.astype(BF16)
    low = (value - high.astype(F32)).astype(BF16)
    return high, low


def mm(a, b):
    return jnp.dot(a, b, preferred_element_type=F32)


def stacked(value):
    high, low = split(value)
    return jnp.concatenate([high, low], axis=0)


def kernel(x_ref, wz, wy, wx, wxi, wyi, out_ref, orb, spec, send, ga, gb, back, vt, ssem, rsem, esem, fsem, bsem, csem, lsem):
    band = lax.axis_index("band")
    grid = lax.axis_index("grid")
    bands = lax.axis_size("band")
    core = grid % 2
    side = band % 2
    mate = (band, grid + 1 - 2 * core)
    near = (band, (grid + 2) % 4)
    cross = (band + 1 - 2 * side, (grid + 2) % 4)
    up = ((band + 2) % bands, grid)
    down = ((band + bands - 2) % bands, grid)
    beyond = (jnp.where(side == 0, up[0], down[0]), grid)

    own_copy = pltpu.make_async_copy(x_ref.at[0], orb.at[OH], lsem)
    own_copy.start()
    barrier = pltpu.get_barrier_semaphore()
    for other in (mate, near, cross, up, down):
        pl.semaphore_signal(barrier, inc=1, device_id=other, device_id_type=MESH)
    pl.semaphore_wait(barrier, 5)

    def remote(src, dst, send_sem, recv_sem, device):
        return pltpu.make_async_remote_copy(
            src_ref=src, dst_ref=dst, send_sem=send_sem, recv_sem=recv_sem, device_id=device, device_id_type=MESH
        )

    moves = {}

    def transfer(index, src, dst, device):
        moves[index] = remote(src, dst, ssem.at[index], rsem.at[index], device)

    def passed_on(index, src_slot, dst_slot, first, count, device):
        rows = pl.ds(first, count)
        transfer(index, orb.at[src_slot, rows], orb.at[dst_slot, rows], device)

    transfer(T_OX, x_ref.at[0], orb.at[OX], near)
    transfer(T_PX, x_ref.at[0], orb.at[PX], cross)
    transfer(T_MH, x_ref.at[0], orb.at[MH], up)
    transfer(T_QH, x_ref.at[0], orb.at[QH], down)
    passed_on(T_MXA, OX, MX, 0, PART, up)
    passed_on(T_MXB, OX, MX, PART, PART, up)
    passed_on(T_QXA, OX, QX, 0, PART, down)
    passed_on(T_QXB, OX, QX, PART, PART, down)
    passed_on(T_PHA, PX, PH, 0, PART, near)
    passed_on(T_PHB, OX, PH, PART, PART, cross)
    passed_on(T_RXZ, PX, RX, ZROWS, Q - ZROWS, beyond)
    passed_on(T_RHZ, PH, RH, ZROWS, Q - ZROWS, beyond)
    far_source = jnp.where(side == 0, QH, MH)
    for k in range(CHUNKS):
        passed_on(T_RX + k, far_source, RX, k * CH, CH, cross)
        passed_on(T_RH + k, RX, RH, k * CH, CH, near)

    block = H * PART
    first_mate = jnp.where(core == 0, 6, 2) * block
    second_mate = jnp.where(core == 0, 2, 6) * block

    def swap(s, part):
        at = (first_mate if part < 2 else second_mate) + (part % 2) * block
        sem = s * 4 + part
        return remote(send.at[s, part], spec.at[s, pl.ds(at, block)], esem.at[sem], fsem.at[sem], mate)

    swaps = {(s, part): swap(s, part) for s in range(SETS) for part in range(4)}
    backs = {
        (turn, c): remote(
            back.at[c], gb.at[turn, c], bsem.at[turn * 2 + c], csem.at[turn * 2 + c], mate
        )
        for turn in range(2)
        for c in range(2)
    }

    def forward(s, o_slot, j_slot, part):
        first = (part % 2) * PART
        keep = (part % 2 + part // 2 * 4) * block

        def step(i, _):
            a = i * 2
            rho = (orb[o_slot, pl.ds(first + a, 2)] * orb[j_slot, pl.ds(first + a, 2)]).reshape(2 * N, N)
            high, low = split(rho)
            t = mm(jnp.concatenate([high, low], axis=1), wz[...])
            t = t[:, :N] + t[:, N:]
            u = mm(wy[core], stacked(jnp.concatenate([t[:N], t[N:]], axis=1)))
            u = u[:N] + u[N:]
            for b in range(2):
                plane = u[:, b * N : b * N + N]
                spec[s, pl.ds(keep + a + b, H, stride=PART), :] = plane[:H]
                send[s, part, pl.ds(a + b, H, stride=PART), :] = plane[H:]
            return 0

        lax.fori_loop(0, PART // 2, step, 0, unroll=UNROLL)
        swaps[s, part].start()

    def row_of(s, k):
        return jnp.concatenate(
            [spec[s, pl.ds(pl.multiple_of(p * block + k * PART, PART), PART), :] for p in range(8)], axis=0
        )

    def along_x(s, turn, c):
        if c == 0:
            column = row_of(s, 0)
            column = column - jnp.where(zero_mode, jnp.mean(column, axis=0, keepdims=True), 0.0)
            for p in range(8):
                spec[s, pl.ds(p * block, PART), :] = column[p * PART : p * PART + PART]

        def step(i, _):
            k = c * (H // 2) + i * 2
            m = jnp.concatenate([row_of(s, k), row_of(s, k + 1)], axis=1)
            f = mm(wx[...], stacked(m))
            v = jnp.concatenate(
                [vt[pl.ds(pl.multiple_of(k * N, N), N), :], vt[pl.ds(pl.multiple_of(k * N + N, N), N), :]], axis=1
            )
            f = (f[:N] + f[N:]) * v
            r = mm(wxi[core], stacked(f))
            r = r[:H] + r[H:]
            for b in range(2):
                plane = r[:, b * N : b * N + N]
                ga[c, pl.ds(i * 2 + b, Q, stride=H // 2), :] = plane[:Q]
                back[c, pl.ds(i * 2 + b, Q, stride=H // 2), :] = plane[Q:]
            return 0

        lax.fori_loop(0, H // 4, step, 0, unroll=UNROLL)
        backs[turn, c].start()

    def inverse(j_slot, turn, first):
        def step(i, _):
            a = i * 2
            planes = []
            for b in range(2):
                rows = pl.ds(pl.multiple_of((a + b) * (H // 2), H // 2), H // 2)
                planes.append(
                    jnp.concatenate([ga[0, rows, :], ga[1, rows, :], gb[turn, 0, rows, :], gb[turn, 1, rows, :]], axis=0)
                )
            t = mm(wyi[core], stacked(jnp.concatenate(planes, axis=1)))
            t = t[:N] + t[N:]
            high, low = split(jnp.concatenate([t[:, :N], t[:, N:]], axis=0))
            w = mm(jnp.concatenate([high, low], axis=1), wz[...])
            w = (w[:, :N] + w[:, N:]).reshape(2, N, N) * orb[j_slot, pl.ds(a, 2)]
            if first:
                out_ref[0, pl.ds(a, 2)] = -w
            else:
                out_ref[0, pl.ds(a, 2)] -= w
            return 0

        lax.fori_loop(0, Q // 2, step, 0, unroll=UNROLL)

    def finish(s, j_slot, turn, between=lambda: None, first=False):
        for part in (2, 3, 0, 1):
            swaps[s, part].wait()
        along_x(s, turn, 0)
        along_x(s, turn, 1)
        between()
        backs[turn, 0].wait()
        backs[turn, 1].wait()
        inverse(j_slot, turn, first)

    def arrived(*indices):
        for t in indices:
            moves[t].wait_recv()

    def start(*indices):
        for t in indices:
            moves[t].start()

    def pass_on(k):
        arrived(T_RX + k)
        start(T_RH + k)

    start(T_OX, T_PX, T_MH, T_QH)

    strength = N * math.sqrt(N) / 16.0 / float(N**3)
    row = lax.broadcasted_iota(jnp.int32, (N, N), 0)
    column = lax.broadcasted_iota(jnp.int32, (N, N), 1)
    row = jnp.minimum(row, N - row)
    column = jnp.minimum(column, N - column)
    plane = row * row + column * column
    zero_mode = jnp.logical_and(lax.broadcasted_iota(jnp.int32, (1, N), 1) == 0, core == 0)

    def table(i, _):
        ky = core * H + i
        ky = jnp.minimum(ky, N - ky)
        d = (plane + ky * ky).astype(F32)
        vt[pl.ds(pl.multiple_of(i * N, N), N), :] = jnp.where(d > 0, strength / jnp.maximum(d, 1.0), 0.0)
        return 0

    lax.fori_loop(0, H, table, 0)
    own_copy.wait()
    forward(0, OH, OH, 0)
    forward(0, OH, OH, 1)

    arrived(T_OX)
    start(T_MXA, T_QXA, T_MXB, T_QXB)
    arrived(T_PX)
    start(T_PHA)
    arrived(T_MH, T_QH)
    start(T_RX, T_RX + 1, T_PHB)
    start(*range(T_RX + 2, T_RX + CHUNKS))
    start(T_RXZ)
    forward(0, OX, OX, 2)
    forward(0, OX, OX, 3)
    finish(0, OH, 0, first=True)
    pass_on(0)
    pass_on(1)
    forward(0, OX, PX, 2)
    forward(0, OX, PX, 3)
    forward(1, OH, MH, 0)
    forward(1, OH, MH, 1)
    forward(2, OH, QH, 0)
    forward(2, OH, QH, 1)
    arrived(T_PHA)
    forward(0, OH, PH, 0)
    arrived(T_MXA)
    forward(1, OX, MX, 2)
    arrived(T_QXA)
    forward(2, OX, QX, 2)
    arrived(T_PHB)
    start(T_RHZ)
    forward(0, OH, PH, 1)
    finish(0, PH, 1, between=lambda: pass_on(2))
    pass_on(3)
    forward(0, OX, RX, 2)
    arrived(T_MXB)
    forward(1, OX, MX, 3)
    finish(1, MH, 0, between=lambda: pass_on(4))
    arrived(T_QXB)
    forward(2, OX, QX, 3)
    finish(2, QH, 1, between=lambda: pass_on(5))
    for k in range(6, CHUNKS):
        pass_on(k)
    arrived(T_RXZ)
    forward(0, OX, RX, 3)
    arrived(*range(T_RH, T_RH + 4))
    forward(0, OH, RH, 0)
    arrived(*range(T_RH + 4, T_RH + CHUNKS), T_RHZ)
    forward(0, OH, RH, 1)
    finish(0, RH, 0)
    for t in range(T_COUNT):
        moves[t].wait_send()


def halves(matrix):
    high = matrix.astype(ml_dtypes.bfloat16)
    low = (matrix - high.astype(np.float64)).astype(ml_dtypes.bfloat16)
    return high, low


def left_weight(matrix):
    high, low = halves(matrix)
    return np.concatenate(
        [np.concatenate([high, high], axis=1), np.concatenate([low, np.zeros_like(low)], axis=1)], axis=0
    )


def tables():
    index = np.arange(N)
    angle = 2.0 * np.pi / N * (index[:, None] * index[None, :] % N)
    cas = np.cos(angle) + np.sin(angle)
    high, low = halves(cas)
    wz = np.concatenate(
        [np.concatenate([high, low], axis=1), np.concatenate([high, np.zeros_like(low)], axis=1)], axis=0
    )
    order = [np.concatenate([index[c * H : c * H + H], index[H - c * H : N - c * H]]) for c in (0, 1)]
    wy = np.stack([left_weight(cas[order[c]]) for c in (0, 1)])
    wyi = np.stack([left_weight(cas[:, order[c]]) for c in (0, 1)])
    wx = left_weight(cas)
    kept = [np.concatenate([index[:Q], index[Q : 2 * Q]]), np.concatenate([index[:Q], index[3 * Q :]])]
    wxi = np.stack([left_weight(cas[kept[c]]) for c in (0, 1)])
    return wz, wy, wx, wxi, wyi


def on_device(orbitals):
    weights = [jnp.asarray(w) for w in tables()]
    vmem = pl.BlockSpec(memory_space=pltpu.VMEM)
    return pl.pallas_call(
        kernel,
        out_shape=jax.ShapeDtypeStruct(orbitals.shape, F32),
        in_specs=[pl.BlockSpec(memory_space=pl.ANY)] + [vmem] * 5,
        out_specs=vmem,
        scratch_shapes=[
            pltpu.VMEM((10, Q, N, N), F32),
            pltpu.VMEM((SETS, N * H, N), F32),
            pltpu.VMEM((SETS, 4, H * PART, N), F32),
            pltpu.VMEM((2, Q * H // 2, N), F32),
            pltpu.VMEM((2, 2, Q * H // 2, N), F32),
            pltpu.VMEM((2, Q * H // 2, N), F32),
            pltpu.VMEM((H * N, N), F32),
            pltpu.SemaphoreType.DMA((T_COUNT,)),
            pltpu.SemaphoreType.DMA((T_COUNT,)),
            pltpu.SemaphoreType.DMA((SETS * 4,)),
            pltpu.SemaphoreType.DMA((SETS * 4,)),
            pltpu.SemaphoreType.DMA((4,)),
            pltpu.SemaphoreType.DMA((4,)),
            pltpu.SemaphoreType.DMA,
        ],
        compiler_params=pltpu.CompilerParams(
            collective_id=0, has_side_effects=True, vmem_limit_bytes=60 * 1024 * 1024
        ),
    )(orbitals, *weights)


def solution(mesh):
    spec = P("band", "grid", None, None)
    return jax.shard_map(on_device, mesh=mesh, in_specs=(spec,), out_specs=spec, check_vma=False)
```

time: 187 us -> 169 us (0.904)
  Pallas kernels: 183 us -> 166 us
    pallas_call x1, Pallas kernels: 183 us -> 166 us  [on_device(): pl.pallas_call(kernel, out_shape=jax.ShapeDtypeStruct(orbitals.shape, F32...]
where the time goes in v3:
time: 169 us
  Pallas kernels  166 us (98%)
  local copies, waits for them, and re-layouts  3.14 us (2%)
    pallas_call x1, Pallas kernels, on_device(): pl.pallas_call(kernel, out_shape=jax.ShapeDtypeStruct(orbitals.shape, F32...  166 us

profile of v3, /device:TPU:1, one launch (start us, length us, event | category | flops | bytes accessed | tf_op | source)
XLA Modules:
  0.0 168.6 jit_solution(15800918999886122683)
XLA Ops:
  0.0 165.5 %shard_map.64 = f32[1,32,128,128]{3,2,1,0:T(8,128)} custom-call(f32[1,32,128,128]{3,2,1,0:T(8,128)} %x_ref.1, bf16[256,256]{1,0:T(8,128)(2,1)} %constant.10.clone.wz, bf16[2,256,256]{2,1,0:T(8,128)(2,1)} %constant.11.clone.wy, bf16[256,256]{1,0:T(8,128)(2,1)} %constant.12.clone.wx, bf16[2,128,256]{2,1,0:T(8,128)(2,1)} %constant.13.clone.wxi, ...), custom_call_target="tpu_custom_call" | custom-call | tf_op jit(solution)/shard_map/pallas_call | solution.py:318
  165.5 3.1 %copy.8 = f32[1,32,128,128]{3,2,1,0:T(8,128)} copy(f32[1,32,128,128]{3,2,1,0:T(8,128)} %shard_map.64) | data formatting | bytes 4194304
